TPU v7x, 512 devices: a whole 4x8x8 slice. The times are simulated.
512 devices in a mesh: grp: 8 (over y_lo, core), tile: 64 (over y_hi, x, z).
Axes of the slice: x: 4, y: 8 (y_hi: 2, y_lo: 4; y = y_hi * 4 + y_lo), z: 8, core: 2. Of those that a mesh axis runs over, the one named last changes fastest.
Arguments:
- hidden: bfloat16 [8, 512, 128, 128], P('grp', 'tile'), may hold values from -13 to 13
- cotangent: float32 [8, 512, 128], P('grp', 'tile'), may hold values from -16 to 16
- spectral_w: bfloat16 [4096, 256], P('tile'), may hold values from -0.375 to 0.375
- conv_k: float32 [9, 128], replicated, may hold values from -2 to 2
- proj_w: float32 [128], replicated, may hold values from -0.5 to 0.5
Outputs:
- grad_hidden: float32 [8, 512, 128, 128], P('grp', 'tile')
- grad_spectral: float32 [4096, 256], P('tile')
- grad_conv: float32 [9, 128], replicated
- grad_proj: float32 [128], replicated
All inputs are finite; a program needn't handle non-finite values.
Results may differ from a plain program's by a relative error of at most 0.015.
Values may be sent and summed in bfloat16 or wider, within the bound.
No kernel may reach another device: no remote copies, remote signals or barrier semaphores. Data moves between devices by JAX's collectives and lax.ppermute only.
A program may use at most 64 MiB of HBM per device.

v0:
```python
import jax
import jax.numpy as jnp
from jax import lax
from jax.sharding import PartitionSpec as P

HIGH = lax.Precision.HIGHEST


def padded(block, sides, width):
    for axis, dim in sides:
        count = lax.axis_size(axis)
        forward = [(i, i + 1) for i in range(count - 1)]
        backward = [(target, source) for source, target in forward]
        low = lax.ppermute(
            lax.slice_in_dim(block, block.shape[dim] - width, None, axis=dim), axis, forward
        )
        high = lax.ppermute(lax.slice_in_dim(block, 0, width, axis=dim), axis, backward)
        block = jnp.concatenate([low, block, high], axis=dim)
    return block


def spectral_tables(modes, bins):
    mode_idx = jnp.arange(modes, dtype=jnp.int32)
    bin_idx = jnp.arange(bins, dtype=jnp.int32)
    phase_int = mode_idx[:, None] * bin_idx[None, :] % bins
    angle_val = phase_int.astype(jnp.float32) * (2.0 * jnp.pi / bins)
    cosine = jnp.cos(angle_val)
    sine = jnp.sin(angle_val)
    forward_tab = jnp.concatenate([cosine, -sine], 0).astype(jnp.bfloat16)
    weight_k = jnp.where(mode_idx == 0, 1.0, 2.0).astype(jnp.float32)[:, None] / bins
    inverse_tab = jnp.concatenate([cosine * weight_k, -sine * weight_k], 0).T.astype(jnp.bfloat16)
    return (forward_tab, inverse_tab)


def build_mixer(weights, modes, chans):
    real_w = weights[:, :chans].reshape(modes, chans, chans)
    imag_w = weights[:, chans:].reshape(modes, chans, chans)
    upper = jnp.concatenate([real_w, imag_w], 2)
    lower = jnp.concatenate([-imag_w, real_w], 2)
    return jnp.concatenate([upper, lower], 1)


def gelu_pair(value):
    normal_cdf = 0.5 * (1.0 + jax.scipy.special.erf(value * 0.7071067811865476))
    return (
        value * normal_cdf,
        normal_cdf + value * jnp.exp(-0.5 * value * value) * 0.3989422804014327,
    )


def cell_backward(hidden_cells, local_term, cot_cells, mixer, forward_tab, inverse_tab, proj_w):
    modes = mixer.shape[0]
    chans = proj_w.shape[0]
    spec_h = jnp.einsum(
        "jb,pbc->jpc", forward_tab, hidden_cells, preferred_element_type=jnp.float32
    ).astype(jnp.bfloat16)
    h_cat = jnp.concatenate([spec_h[:modes], spec_h[modes:]], 2)
    mixed = jnp.einsum("kpa,kab->kpb", h_cat, mixer, preferred_element_type=jnp.float32).astype(
        jnp.bfloat16
    )
    mixed_stack = jnp.concatenate([mixed[:, :, :chans], mixed[:, :, chans:]], 0)
    spectral_out = jnp.einsum(
        "bj,jpo->pbo", inverse_tab, mixed_stack, preferred_element_type=jnp.float32
    )
    pre_act = spectral_out + local_term
    activ, slope = gelu_pair(pre_act)
    proj_grad = jnp.einsum("pb,pbo->o", cot_cells, activ, precision=HIGH)
    grad_pre = (cot_cells[:, :, None] * proj_w * slope).astype(jnp.bfloat16)
    grad_mix = jnp.einsum(
        "bj,pbo->jpo", inverse_tab, grad_pre, preferred_element_type=jnp.float32
    ).astype(jnp.bfloat16)
    grad_real = grad_mix[:modes]
    grad_imag = grad_mix[modes:]
    grad_cat = jnp.concatenate([grad_real, grad_imag], 2)
    grad_spec = jnp.einsum(
        "kpb,kab->kpa", grad_cat, mixer, preferred_element_type=jnp.float32
    ).astype(jnp.bfloat16)
    grad_stack = jnp.concatenate([grad_spec[:, :, :chans], grad_spec[:, :, chans:]], 0)
    grad_in = jnp.einsum("jb,jpc->pbc", forward_tab, grad_stack, preferred_element_type=jnp.float32)
    left_side = jnp.concatenate([spec_h[:modes], spec_h[modes:]], 1)
    right_side = jnp.concatenate([grad_cat, jnp.concatenate([grad_imag, -grad_real], 2)], 1)
    weight_term = jnp.einsum(
        "kpc,kpo->kco", left_side, right_side, preferred_element_type=jnp.float32
    ).reshape(modes * chans, 2 * chans)
    return (grad_pre, grad_in, weight_term, proj_grad)


def local(hidden, cotangent, spectral_w, conv_k, proj_w):
    rows_here, cols_here, bins_here, chans = hidden.shape
    modes = spectral_w.shape[0] * lax.axis_size("tile") // chans
    cell_count = rows_here * cols_here
    forward_tab, inverse_tab = spectral_tables(modes, bins_here)
    x_pad = padded(hidden, (("grp", 0), ("tile", 1)), 1)
    offsets = [(row_off, col_off) for row_off in (-1, 0, 1) for col_off in (-1, 0, 1)]
    local_term = jnp.zeros((rows_here, cols_here, bins_here, chans), jnp.float32)
    for index_d, (row_off, col_off) in enumerate(offsets):
        window = x_pad[1 + row_off : 1 + row_off + rows_here, 1 + col_off : 1 + col_off + cols_here]
        local_term = local_term + window.astype(jnp.float32) * conv_k[index_d]
    whole_w = lax.all_gather(spectral_w, "tile", axis=0, tiled=True)
    mixer = build_mixer(whole_w, modes, chans)
    grad_pre, grad_in, weight_term, proj_grad = cell_backward(
        hidden.reshape(cell_count, bins_here, chans),
        local_term.reshape(cell_count, bins_here, chans),
        cotangent.reshape(cell_count, bins_here),
        mixer,
        forward_tab,
        inverse_tab,
        proj_w,
    )
    grad_block = grad_pre.reshape(rows_here, cols_here, bins_here, chans)
    conv_part = jnp.stack(
        [
            jnp.einsum(
                "xybc,xybc->c",
                x_pad[1 + row_off : 1 + row_off + rows_here, 1 + col_off : 1 + col_off + cols_here],
                grad_block,
                preferred_element_type=jnp.float32,
            )
            for row_off, col_off in offsets
        ],
        0,
    )
    grad_pad = padded(grad_block, (("grp", 0), ("tile", 1)), 1)
    grad_hidden = grad_in.reshape(rows_here, cols_here, bins_here, chans)
    for index_d, (row_off, col_off) in enumerate(offsets):
        window = grad_pad[
            1 - row_off : 1 - row_off + rows_here, 1 - col_off : 1 - col_off + cols_here
        ]
        grad_hidden = grad_hidden + window.astype(jnp.float32) * conv_k[index_d]
    tile_share = lax.psum_scatter(weight_term, "tile", scatter_dimension=0, tiled=True)
    grad_spectral = lax.psum(tile_share.astype(jnp.bfloat16), "grp").astype(jnp.float32)
    conv_all, proj_all = lax.psum((conv_part, proj_grad), ("grp", "tile"))
    return (grad_hidden, grad_spectral, conv_all, proj_all)


def solution(mesh):
    in_specs = (P("grp", "tile", None, None), P("grp", "tile", None), P("tile", None), P(), P())
    out_specs = (P("grp", "tile", None, None), P("tile", None), P(), P())
    return jax.shard_map(local, mesh=mesh, in_specs=in_specs, out_specs=out_specs, check_vma=False)
```

profile of v0, /device:TPU:1, one launch (start us, length us, event | category | flops | bytes accessed | tf_op | source)
XLA Modules:
  0.0 639.4 jit_solution(11236863667525213482)
XLA Ops:
  7.2 0.0 all-gather.2.cloned.1.call-start
  7.2 0.7 all-gather.2.cloned.1.call-update
  7.9 0.0 reduce-scatter.2.cloned.1.call-start
  7.9 1.1 copy.11
  9.1 8.8 %collective-permute-start.1 = (bf16[1,8,128,128]{2,3,1,0:T(8,128)(2,1)S(1)}, bf16[1,8,128,128]{2,3,1,0:T(8,128)(2,1)S(1)}, u32[]{:S(2)}, u32[]{:S(2)}) collective-permute-start(bf16[1,8,128,128]{2,3,1,0:T(8,128)(2,1)S(1)} %copy.11), channel_id=1, source_target_pairs={{64,0},{128,64},{192,128},{256,192},{320,256},{384,320},{448,384},... | collective-permute-start | bytes 786440 | tf_op jit(solution)/shard_map/ppermute | solution.py:17
  17.9 1.9 collective-permute-start
  19.8 0.1 fusion.41
  19.9 1.1 convolution_convert_fusion.1
  21.1 1.0 slice_bitcast_fusion.8
  22.1 0.0 copy-start.11
  22.2 0.1 multiply_convert_fusion.1
  22.3 0.8 collective-permute-done
  23.1 1.3 collective-permute-start.3
  24.4 4.0 collective-permute-start.2
  28.4 119.3 %all-gather.2.cloned.1.call-done = bf16[4096,256]{1,0:T(8,128)(2,1)} async-done(((bf16[64,256]{1,0:T(8,128)(2,1)}), bf16[4096,256]{1,0:T(8,128)(2,1)}) %all-gather.2.cloned.1.call-update) | async-done | bytes 2097168 | tf_op jit(solution)/shard_map/all_gather | solution.py:99
  147.7 1.7 fusion.52
  149.4 0.3 neg.13
  149.7 0.0 copy-start.23
  149.7 0.0 copy-start.25
  149.7 0.9 fusion.2
  150.6 0.2 copy-done.1
  150.9 1.6 bitcast_convert_fusion
  152.5 0.2 convolution_convert_fusion
  152.8 0.0 copy-start
  152.8 2.7 fusion.24
  155.5 0.0 reduce-scatter.2.cloned.1.call-update
  155.5 6.4 %collective-permute-start.5 = (bf16[1,8,128,128]{2,3,1,0:T(8,128)(2,1)S(1)}, bf16[1,8,128,128]{2,3,1,0:T(8,128)(2,1)}, u32[]{:S(2)}, u32[]{:S(2)}) collective-permute-start(bf16[1,8,128,128]{2,3,1,0:T(8,128)(2,1)S(1)} %bitcast.128), channel_id=1, source_target_pairs={{64,0},{128,64},{192,128},{256,192},{320,256},{384,320},{448,384},... | collective-permute-start | bytes 786440 | tf_op jit(solution)/shard_map/ppermute | solution.py:17
  161.9 5.1 collective-permute-start.4
  167.0 0.2 copy.51
  167.2 0.2 multiply_reduce_fusion
  167.4 1.0 fusion.14
  168.4 1.2 fusion.15
  169.6 0.0 copy-start.26
  169.6 0.0 copy-start.12
  169.7 3.2 fusion.3
  172.9 0.6 convolution_bitcast_fusion.2
  173.5 97.4 %all-reduce = (f32[9,128]{1,0:T(8,128)}, f32[128]{0:T(128)}) all-reduce(f32[9,128]{1,0:T(8,128)S(1)} %stack.39, f32[128]{0:T(128)S(1)} %convolution_bitcast_fusion.2), channel_id=1, replica_groups=mesh['grp'=8,'tile'=64] {'grp','tile'}, use_global_device_ids=true, to_apply=%region_2.3 | all-reduce | flops 1280 | bytes 10240 | tf_op jit(solution)/shard_map/psum | solution.py:132
  270.9 0.8 pad_maximum_fusion.23
  271.8 1.3 collective-permute-start.6
  273.1 4.0 collective-permute-start.7
  277.1 0.4 collective-permute-done.6
  277.5 1.3 collective-permute-done.7
  278.9 2.1 fusion.21
  281.1 1.0 copy.20
  282.1 273.8 %reduce-scatter.2.cloned.1.call-done = f32[64,256]{1,0:T(8,128)} async-done(((f32[4096,256]{1,0:T(8,128)}), f32[64,256]{1,0:T(8,128)}) %reduce-scatter.2.cloned.1.call-update) | async-done | bytes 65552 | tf_op jit(solution)/shard_map/reduce_scatter | solution.py:130
  555.8 0.8 convert_element_type.112
  556.7 75.3 %psum.21 = bf16[64,256]{1,0:T(8,128)(2,1)S(1)} all-reduce(bf16[64,256]{1,0:T(8,128)(2,1)S(1)} %convert_element_type.112), channel_id=1, replica_groups=mesh['grp'=8,'tile'=64] {'grp'}, use_global_device_ids=true, to_apply=%region_1.2 | all-reduce | flops 16384 | bytes 65536 | tf_op jit(solution)/shard_map/psum | solution.py:131
  632.0 0.6 convert_element_type.113
  (65 shorter events, 0.3 us)
Async XLA Ops:
  7.2 140.5 %all-gather.2.cloned.1.call-start = ((), (), s32[]{:S(2)}) async-start(), calls=%async_computation.1 | async-start | bytes 2129920 | tf_op jit(solution)/shard_map/all_gather | solution.py:99
  7.9 548.0 %reduce-scatter.2.cloned.1.call-start = ((), (), s32[]{:S(2)}) async-start(), calls=%async_computation.2 | async-start | bytes 4259840 | tf_op jit(solution)/shard_map/reduce_scatter | solution.py:130
  9.1 13.2 %collective-permute-start.1 = (bf16[1,8,128,128]{2,3,1,0:T(8,128)(2,1)S(1)}, bf16[1,8,128,128]{2,3,1,0:T(8,128)(2,1)S(1)}, u32[]{:S(2)}, u32[]{:S(2)}) collective-permute-start(bf16[1,8,128,128]{2,3,1,0:T(8,128)(2,1)S(1)} %copy.11), channel_id=1, source_target_pairs={{64,0},{128,64},{192,128},{256,192},{320,256},{384,320},{448,384},... | collective-permute-start | bytes 786440 | tf_op jit(solution)/shard_map/ppermute | solution.py:17
  17.9 5.2 collective-permute-start
  22.1 128.7 %copy-start.5 = (f32[128]{0:T(128)}, f32[128]{0:T(128)S(1)}, u32[]{:S(2)}) copy-start(f32[128]{0:T(128)S(1)} %get-tuple-element.35) | copy-start | bytes 1540
  22.1 128.7 %copy-start.7 = (f32[128]{0:T(128)}, f32[128]{0:T(128)S(1)}, u32[]{:S(2)}) copy-start(f32[128]{0:T(128)S(1)} %get-tuple-element.36) | copy-start | bytes 1540
  22.1 128.7 %copy-start.9 = (f32[128]{0:T(128)}, f32[128]{0:T(128)S(1)}, u32[]{:S(2)}) copy-start(f32[128]{0:T(128)S(1)} %get-tuple-element.37) | copy-start | bytes 1540
  22.1 128.7 %copy-start.11 = (f32[128]{0:T(128)}, f32[128]{0:T(128)S(1)}, u32[]{:S(2)}) copy-start(f32[128]{0:T(128)S(1)} %get-tuple-element.38) | copy-start | bytes 1540
  22.1 128.7 %copy-start.13 = (f32[128]{0:T(128)}, f32[128]{0:T(128)S(1)}, u32[]{:S(2)}) copy-start(f32[128]{0:T(128)S(1)} %get-tuple-element.39) | copy-start | bytes 1540
  22.1 128.7 %copy-start.15 = (f32[128]{0:T(128)}, f32[128]{0:T(128)S(1)}, u32[]{:S(2)}) copy-start(f32[128]{0:T(128)S(1)} %get-tuple-element.40) | copy-start | bytes 1540
  22.1 128.7 %copy-start.17 = (f32[128]{0:T(128)}, f32[128]{0:T(128)S(1)}, u32[]{:S(2)}) copy-start(f32[128]{0:T(128)S(1)} %get-tuple-element.41) | copy-start | bytes 1540
  22.1 128.7 %copy-start.19 = (f32[128]{0:T(128)}, f32[128]{0:T(128)S(1)}, u32[]{:S(2)}) copy-start(f32[128]{0:T(128)S(1)} %get-tuple-element.42) | copy-start | bytes 1540
  22.2 128.7 %copy-start.21 = (f32[128]{0:T(128)}, f32[128]{0:T(128)S(1)}, u32[]{:S(2)}) copy-start(f32[128]{0:T(128)S(1)} %get-tuple-element.43) | copy-start | bytes 1540
  23.1 127.7 %collective-permute-start.3 = (bf16[3,1,128,128]{2,3,1,0:T(8,128)(2,1)S(1)}, bf16[3,1,128,128]{2,3,1,0:T(8,128)(2,1)S(1)}, u32[]{:S(2)}, u32[]{:S(2)}) collective-permute-start(bf16[3,1,128,128]{2,3,1,0:T(8,128)(2,1)S(1)} %get-tuple-element.24), channel_id=1, source_target_pairs={{1,0},{2,1},{3,2},{4,3},{5,4},{6,5},{7,6},{8,7},{9,8},{10,9},{11,1... | collective-permute-start | bytes 294920 | tf_op jit(solution)/shard_map/ppermute | solution.py:17
  24.4 126.4 %collective-permute-start.2 = (bf16[3,1,128,128]{2,3,1,0:T(8,128)(2,1)S(1)}, bf16[3,1,128,128]{2,3,1,0:T(8,128)(2,1)S(1)}, u32[]{:S(2)}, u32[]{:S(2)}) collective-permute-start(bf16[3,1,128,128]{2,3,1,0:T(8,128)(2,1)S(1)} %get-tuple-element.25), channel_id=1, source_target_pairs={{0,1},{1,2},{2,3},{3,4},{4,5},{5,6},{6,7},{7,8},{8,9},{9,10},{10,1... | collective-permute-start | bytes 294920 | tf_op jit(solution)/shard_map/ppermute | solution.py:14
  149.4 1.2 copy-start.2
  149.7 1.1 copy-start.1
  149.7 1.2 copy-start.23
  149.7 1.2 copy-start.25
  150.8 1.7 copy-start.3
  150.8 1.7 copy-start.4
  152.8 14.5 %copy-start = (bf16[1,8,128,128]{3,2,1,0:T(8,128)(2,1)S(1)}, bf16[1,8,128,128]{3,2,1,0:T(8,128)(2,1)}, u32[]{:S(2)}) copy-start(bf16[1,8,128,128]{3,2,1,0:T(8,128)(2,1)} %param.5) | copy-start | bytes 786436
  155.5 115.4 %collective-permute-start.5 = (bf16[1,8,128,128]{2,3,1,0:T(8,128)(2,1)S(1)}, bf16[1,8,128,128]{2,3,1,0:T(8,128)(2,1)}, u32[]{:S(2)}, u32[]{:S(2)}) collective-permute-start(bf16[1,8,128,128]{2,3,1,0:T(8,128)(2,1)S(1)} %bitcast.128), channel_id=1, source_target_pairs={{64,0},{128,64},{192,128},{256,192},{320,256},{384,320},{448,384},... | collective-permute-start | bytes 786440 | tf_op jit(solution)/shard_map/ppermute | solution.py:17
  161.9 109.0 %collective-permute-start.4 = (bf16[1,8,128,128]{2,3,1,0:T(8,128)(2,1)S(1)}, bf16[1,8,128,128]{2,3,1,0:T(8,128)(2,1)}, u32[]{:S(2)}, u32[]{:S(2)}) collective-permute-start(bf16[1,8,128,128]{2,3,1,0:T(8,128)(2,1)S(1)} %bitcast.129), channel_id=1, source_target_pairs={{0,64},{64,128},{128,192},{192,256},{256,320},{320,384},{384,448},... | collective-permute-start | bytes 786440 | tf_op jit(solution)/shard_map/ppermute | solution.py:14
  169.6 3.3 copy-start.24
  169.6 3.3 copy-start.26
  169.6 109.2 %copy-start.6 = (f32[128]{0:T(128)S(1)}, f32[128]{0:T(128)}, u32[]{:S(2)}) copy-start(f32[128]{0:T(128)} %copy-done.5) | copy-start | bytes 1540
  169.6 109.2 %copy-start.8 = (f32[128]{0:T(128)S(1)}, f32[128]{0:T(128)}, u32[]{:S(2)}) copy-start(f32[128]{0:T(128)} %copy-done.7) | copy-start | bytes 1540
  169.6 109.2 %copy-start.10 = (f32[128]{0:T(128)S(1)}, f32[128]{0:T(128)}, u32[]{:S(2)}) copy-start(f32[128]{0:T(128)} %copy-done.9) | copy-start | bytes 1540
  169.6 109.2 %copy-start.12 = (f32[128]{0:T(128)S(1)}, f32[128]{0:T(128)}, u32[]{:S(2)}) copy-start(f32[128]{0:T(128)} %copy-done.11) | copy-start | bytes 1540
  169.7 109.2 %copy-start.14 = (f32[128]{0:T(128)S(1)}, f32[128]{0:T(128)}, u32[]{:S(2)}) copy-start(f32[128]{0:T(128)} %copy-done.13) | copy-start | bytes 1540
  169.7 109.2 %copy-start.16 = (f32[128]{0:T(128)S(1)}, f32[128]{0:T(128)}, u32[]{:S(2)}) copy-start(f32[128]{0:T(128)} %copy-done.15) | copy-start | bytes 1540
  169.7 109.2 %copy-start.18 = (f32[128]{0:T(128)S(1)}, f32[128]{0:T(128)}, u32[]{:S(2)}) copy-start(f32[128]{0:T(128)} %copy-done.17) | copy-start | bytes 1540
  169.7 109.2 %copy-start.20 = (f32[128]{0:T(128)S(1)}, f32[128]{0:T(128)}, u32[]{:S(2)}) copy-start(f32[128]{0:T(128)} %copy-done.19) | copy-start | bytes 1540
  169.7 109.2 %copy-start.22 = (f32[128]{0:T(128)S(1)}, f32[128]{0:T(128)}, u32[]{:S(2)}) copy-start(f32[128]{0:T(128)} %copy-done.21) | copy-start | bytes 1540
  271.8 5.8 collective-permute-start.6
  273.1 5.8 collective-permute-start.7
Sparse Core Ops, SparseCore 0:
  12.6 135.0 all-gather.1
  155.6 400.1 reduce-scatter.1
where the time goes:
time: 640 us; the launch traced here: 639 us
  waiting for transfers between devices  396 us (62%)
  blocking collectives  173 us (27%)
  starting transfers between devices  32.8 us (5%)
  between operations  14.6 us (2%)
  matrix products  12.4 us (2%)
    reduce_scatter x1, waiting for transfers between devices, local(): lax.psum_scatter(weight_term, 'tile', scatter_dimension=0, tiled=True)  274 us
    all_gather x1, waiting for transfers between devices, local(): whole_w = lax.all_gather(spectral_w, 'tile', axis=0, tiled=True)  119 us
    psum x1, blocking collectives, local(): conv_all, proj_all = lax.psum((conv_part, proj_grad), ('grp', 'tile'))  97.4 us
    psum x1, blocking collectives, local(): lax.psum(tile_share.astype(jnp.bfloat16), 'grp').astype(jnp.float32)  75.3 us
    ppermute x4, starting transfers between devices, padded(): lax.ppermute(lax.slice_in_dim(block, 0, width, axis=dim), axis, backward)  17.8 us
    ppermute x4, starting transfers between devices, padded(): lax.ppermute(lax.slice_in_dim(block, block.shape[dim] - width, None, axis...  15 us
  transfers between devices with their start and end apart: 10, of which 5 were waited for; matrix products, arithmetic and copies ran while one was open for 3% of the time, Pallas kernels for 0%

commit v1 on v0

--- a/solution.py
+++ b/solution.py
@@ -129,7 +129,7 @@
         grad_hidden = grad_hidden + window.astype(jnp.float32) * conv_k[index_d]
     tile_share = lax.psum_scatter(weight_term, "tile", scatter_dimension=0, tiled=True)
     grad_spectral = lax.psum(tile_share.astype(jnp.bfloat16), "grp").astype(jnp.float32)
-    conv_all, proj_all = lax.psum((conv_part, proj_grad), ("grp", "tile"))
+    conv_all, proj_all = lax.psum(lax.psum((conv_part, proj_grad), "grp"), "tile")
     return (grad_hidden, grad_spectral, conv_all, proj_all)
 
 

time: 640 us -> 641 us (level)
  blocking collectives: 173 us -> 282 us
  waiting for transfers between devices: 396 us -> 288 us
    psum x1 -> x2, blocking collectives: 97.4 us -> 209 us  [the longest x1 197 us: local(): lax.psum(lax.psum((conv_part, proj_grad), 'grp'), 'tile')]
    reduce_scatter x1, waiting for transfers between devices: 274 us -> 166 us  [local(): lax.psum_scatter(weight_term, 'tile', scatter_dimension=0, tiled=True)]
where the time goes in v1:
time: 641 us; the launch traced here: 640 us
  waiting for transfers between devices  288 us (45%)
  blocking collectives  282 us (44%)
  starting transfers between devices  32.8 us (5%)
  between operations  14.7 us (2%)
  matrix products  12.3 us (2%)
    psum x1, blocking collectives, local(): lax.psum(lax.psum((conv_part, proj_grad), 'grp'), 'tile')  197 us
    reduce_scatter x1, waiting for transfers between devices, local(): lax.psum_scatter(weight_term, 'tile', scatter_dimension=0, tiled=True)  166 us
    all_gather x1, waiting for transfers between devices, local(): whole_w = lax.all_gather(spectral_w, 'tile', axis=0, tiled=True)  119 us
    psum x1, blocking collectives, local(): lax.psum(tile_share.astype(jnp.bfloat16), 'grp').astype(jnp.float32)  72.5 us
    ppermute x4, starting transfers between devices, padded(): lax.ppermute(lax.slice_in_dim(block, 0, width, axis=dim), axis, backward)  17.8 us
    ppermute x4, starting transfers between devices, padded(): lax.ppermute(lax.slice_in_dim(block, block.shape[dim] - width, None, axis...  15 us
  transfers between devices with their start and end apart: 10, of which 5 were waited for; matrix products, arithmetic and copies ran while one was open for 3% of the time, Pallas kernels for 0%

profile of v1, /device:TPU:1, one launch (start us, length us, event | category | flops | bytes accessed | tf_op | source)
XLA Modules:
  0.0 640.0 jit_solution(3420835751443176134)
XLA Ops:
  7.2 0.0 all-gather.2.cloned.1.call-start
  7.2 0.7 all-gather.2.cloned.1.call-update
  7.9 0.0 reduce-scatter.2.cloned.1.call-start
  7.9 1.1 copy.11
  9.1 8.8 %collective-permute-start.1 = (bf16[1,8,128,128]{2,3,1,0:T(8,128)(2,1)S(1)}, bf16[1,8,128,128]{2,3,1,0:T(8,128)(2,1)S(1)}, u32[]{:S(2)}, u32[]{:S(2)}) collective-permute-start(bf16[1,8,128,128]{2,3,1,0:T(8,128)(2,1)S(1)} %copy.11), channel_id=1, source_target_pairs={{64,0},{128,64},{192,128},{256,192},{320,256},{384,320},{448,384},... | collective-permute-start | bytes 786440 | tf_op jit(solution)/shard_map/ppermute | solution.py:17
  17.9 1.9 collective-permute-start
  19.8 0.1 fusion.41
  19.9 1.1 convolution_convert_fusion.1
  21.1 1.0 slice_bitcast_fusion.8
  22.1 0.0 copy-start.11
  22.2 0.1 multiply_convert_fusion.1
  22.3 0.8 collective-permute-done
  23.1 1.3 collective-permute-start.3
  24.4 4.0 collective-permute-start.2
  28.4 119.3 %all-gather.2.cloned.1.call-done = bf16[4096,256]{1,0:T(8,128)(2,1)} async-done(((bf16[64,256]{1,0:T(8,128)(2,1)}), bf16[4096,256]{1,0:T(8,128)(2,1)}) %all-gather.2.cloned.1.call-update) | async-done | bytes 2097168 | tf_op jit(solution)/shard_map/all_gather | solution.py:99
  147.7 1.7 fusion.52
  149.4 0.3 neg.13
  149.7 0.0 copy-start.23
  149.7 0.0 copy-start.25
  149.7 0.9 fusion.2
  150.6 0.1 copy-done.1
  150.9 1.6 bitcast_convert_fusion
  152.5 0.2 convolution_convert_fusion
  152.8 0.0 copy-start
  152.8 2.7 fusion.24
  155.5 0.0 reduce-scatter.2.cloned.1.call-update
  155.5 6.4 %collective-permute-start.5 = (bf16[1,8,128,128]{2,3,1,0:T(8,128)(2,1)S(1)}, bf16[1,8,128,128]{2,3,1,0:T(8,128)(2,1)}, u32[]{:S(2)}, u32[]{:S(2)}) collective-permute-start(bf16[1,8,128,128]{2,3,1,0:T(8,128)(2,1)S(1)} %bitcast.128), channel_id=1, source_target_pairs={{64,0},{128,64},{192,128},{256,192},{320,256},{384,320},{448,384},... | collective-permute-start | bytes 786440 | tf_op jit(solution)/shard_map/ppermute | solution.py:17
  161.9 5.1 collective-permute-start.4
  167.0 0.2 copy.51
  167.2 0.2 multiply_reduce_fusion
  167.4 1.0 fusion.14
  168.4 1.2 fusion.15
  169.6 0.0 copy-start.26
  169.7 3.2 fusion.3
  172.9 0.6 convolution_bitcast_fusion.2
  173.5 11.8 %all-reduce.1 = (f32[9,128]{1,0:T(8,128)S(1)}, f32[128]{0:T(128)S(1)}) all-reduce(f32[9,128]{1,0:T(8,128)S(1)} %stack.39, f32[128]{0:T(128)S(1)} %convolution_bitcast_fusion.2), channel_id=1, replica_groups=mesh['grp'=8,'tile'=64] {'grp'}, use_global_device_ids=true, to_apply=%region_2.3 | all-reduce | flops 1280 | bytes 10240 | tf_op jit(solution)/shard_map/psum | solution.py:132
  185.3 197.2 %all-reduce = (f32[9,128]{1,0:T(8,128)}, f32[128]{0:T(128)}) all-reduce(f32[9,128]{1,0:T(8,128)S(1)} %get-tuple-element.18, f32[128]{0:T(128)S(1)} %get-tuple-element.19), channel_id=1, replica_groups=mesh['grp'=8,'tile'=64] {'tile'}, use_global_device_ids=true, to_apply=%region_3.4 | all-reduce | flops 1280 | bytes 10240 | tf_op jit(solution)/shard_map/psum | solution.py:132
  382.6 0.8 pad_maximum_fusion.23
  383.4 1.3 collective-permute-start.6
  384.7 4.0 collective-permute-start.7
  388.8 0.4 collective-permute-done.6
  389.2 1.3 collective-permute-done.7
  390.5 2.1 fusion.21
  392.6 1.0 copy.20
  393.6 165.5 %reduce-scatter.2.cloned.1.call-done = f32[64,256]{1,0:T(8,128)} async-done(((f32[4096,256]{1,0:T(8,128)}), f32[64,256]{1,0:T(8,128)}) %reduce-scatter.2.cloned.1.call-update) | async-done | bytes 65552 | tf_op jit(solution)/shard_map/reduce_scatter | solution.py:130
  559.1 0.8 convert_element_type.112
  560.0 72.5 %psum.35 = bf16[64,256]{1,0:T(8,128)(2,1)S(1)} all-reduce(bf16[64,256]{1,0:T(8,128)(2,1)S(1)} %convert_element_type.112), channel_id=1, replica_groups=mesh['grp'=8,'tile'=64] {'grp'}, use_global_device_ids=true, to_apply=%region_1.2 | all-reduce | flops 16384 | bytes 65536 | tf_op jit(solution)/shard_map/psum | solution.py:131
  632.5 0.6 convert_element_type.113
  (66 shorter events, 0.4 us)
Async XLA Ops:
  7.2 140.5 %all-gather.2.cloned.1.call-start = ((), (), s32[]{:S(2)}) async-start(), calls=%async_computation.1 | async-start | bytes 2129920 | tf_op jit(solution)/shard_map/all_gather | solution.py:99
  7.9 551.2 %reduce-scatter.2.cloned.1.call-start = ((), (), s32[]{:S(2)}) async-start(), calls=%async_computation.2 | async-start | bytes 4259840 | tf_op jit(solution)/shard_map/reduce_scatter | solution.py:130
  9.1 13.2 %collective-permute-start.1 = (bf16[1,8,128,128]{2,3,1,0:T(8,128)(2,1)S(1)}, bf16[1,8,128,128]{2,3,1,0:T(8,128)(2,1)S(1)}, u32[]{:S(2)}, u32[]{:S(2)}) collective-permute-start(bf16[1,8,128,128]{2,3,1,0:T(8,128)(2,1)S(1)} %copy.11), channel_id=1, source_target_pairs={{64,0},{128,64},{192,128},{256,192},{320,256},{384,320},{448,384},... | collective-permute-start | bytes 786440 | tf_op jit(solution)/shard_map/ppermute | solution.py:17
  17.9 5.2 collective-permute-start
  22.1 128.7 %copy-start.5 = (f32[128]{0:T(128)}, f32[128]{0:T(128)S(1)}, u32[]{:S(2)}) copy-start(f32[128]{0:T(128)S(1)} %get-tuple-element.37) | copy-start | bytes 1540
  22.1 128.7 %copy-start.7 = (f32[128]{0:T(128)}, f32[128]{0:T(128)S(1)}, u32[]{:S(2)}) copy-start(f32[128]{0:T(128)S(1)} %get-tuple-element.38) | copy-start | bytes 1540
  22.1 128.7 %copy-start.9 = (f32[128]{0:T(128)}, f32[128]{0:T(128)S(1)}, u32[]{:S(2)}) copy-start(f32[128]{0:T(128)S(1)} %get-tuple-element.39) | copy-start | bytes 1540
  22.1 128.7 %copy-start.11 = (f32[128]{0:T(128)}, f32[128]{0:T(128)S(1)}, u32[]{:S(2)}) copy-start(f32[128]{0:T(128)S(1)} %get-tuple-element.40) | copy-start | bytes 1540
  22.1 128.7 %copy-start.13 = (f32[128]{0:T(128)}, f32[128]{0:T(128)S(1)}, u32[]{:S(2)}) copy-start(f32[128]{0:T(128)S(1)} %get-tuple-element.41) | copy-start | bytes 1540
  22.1 128.7 %copy-start.15 = (f32[128]{0:T(128)}, f32[128]{0:T(128)S(1)}, u32[]{:S(2)}) copy-start(f32[128]{0:T(128)S(1)} %get-tuple-element.42) | copy-start | bytes 1540
  22.1 128.7 %copy-start.17 = (f32[128]{0:T(128)}, f32[128]{0:T(128)S(1)}, u32[]{:S(2)}) copy-start(f32[128]{0:T(128)S(1)} %get-tuple-element.43) | copy-start | bytes 1540
  22.1 128.7 %copy-start.19 = (f32[128]{0:T(128)}, f32[128]{0:T(128)S(1)}, u32[]{:S(2)}) copy-start(f32[128]{0:T(128)S(1)} %get-tuple-element.44) | copy-start | bytes 1540
  22.2 128.7 %copy-start.21 = (f32[128]{0:T(128)}, f32[128]{0:T(128)S(1)}, u32[]{:S(2)}) copy-start(f32[128]{0:T(128)S(1)} %get-tuple-element.45) | copy-start | bytes 1540
  23.1 127.6 %collective-permute-start.3 = (bf16[3,1,128,128]{2,3,1,0:T(8,128)(2,1)S(1)}, bf16[3,1,128,128]{2,3,1,0:T(8,128)(2,1)S(1)}, u32[]{:S(2)}, u32[]{:S(2)}) collective-permute-start(bf16[3,1,128,128]{2,3,1,0:T(8,128)(2,1)S(1)} %get-tuple-element.26), channel_id=1, source_target_pairs={{1,0},{2,1},{3,2},{4,3},{5,4},{6,5},{7,6},{8,7},{9,8},{10,9},{11,1... | collective-permute-start | bytes 294920 | tf_op jit(solution)/shard_map/ppermute | solution.py:17
  24.4 126.4 %collective-permute-start.2 = (bf16[3,1,128,128]{2,3,1,0:T(8,128)(2,1)S(1)}, bf16[3,1,128,128]{2,3,1,0:T(8,128)(2,1)S(1)}, u32[]{:S(2)}, u32[]{:S(2)}) collective-permute-start(bf16[3,1,128,128]{2,3,1,0:T(8,128)(2,1)S(1)} %get-tuple-element.27), channel_id=1, source_target_pairs={{0,1},{1,2},{2,3},{3,4},{4,5},{5,6},{6,7},{7,8},{8,9},{9,10},{10,1... | collective-permute-start | bytes 294920 | tf_op jit(solution)/shard_map/ppermute | solution.py:14
  149.4 1.2 copy-start.2
  149.7 1.1 copy-start.1
  149.7 1.2 copy-start.23
  149.7 1.2 copy-start.25
  150.8 1.7 copy-start.3
  150.8 1.7 copy-start.4
  152.8 14.5 %copy-start = (bf16[1,8,128,128]{3,2,1,0:T(8,128)(2,1)S(1)}, bf16[1,8,128,128]{3,2,1,0:T(8,128)(2,1)}, u32[]{:S(2)}) copy-start(bf16[1,8,128,128]{3,2,1,0:T(8,128)(2,1)} %param.5) | copy-start | bytes 786436
  155.5 227.1 %collective-permute-start.5 = (bf16[1,8,128,128]{2,3,1,0:T(8,128)(2,1)S(1)}, bf16[1,8,128,128]{2,3,1,0:T(8,128)(2,1)}, u32[]{:S(2)}, u32[]{:S(2)}) collective-permute-start(bf16[1,8,128,128]{2,3,1,0:T(8,128)(2,1)S(1)} %bitcast.128), channel_id=1, source_target_pairs={{64,0},{128,64},{192,128},{256,192},{320,256},{384,320},{448,384},... | collective-permute-start | bytes 786440 | tf_op jit(solution)/shard_map/ppermute | solution.py:17
  161.9 220.7 %collective-permute-start.4 = (bf16[1,8,128,128]{2,3,1,0:T(8,128)(2,1)S(1)}, bf16[1,8,128,128]{2,3,1,0:T(8,128)(2,1)}, u32[]{:S(2)}, u32[]{:S(2)}) collective-permute-start(bf16[1,8,128,128]{2,3,1,0:T(8,128)(2,1)S(1)} %bitcast.129), channel_id=1, source_target_pairs={{0,64},{64,128},{128,192},{192,256},{256,320},{320,384},{384,448},... | collective-permute-start | bytes 786440 | tf_op jit(solution)/shard_map/ppermute | solution.py:14
  169.6 3.3 copy-start.24
  169.6 3.3 copy-start.26
  169.6 220.9 %copy-start.6 = (f32[128]{0:T(128)S(1)}, f32[128]{0:T(128)}, u32[]{:S(2)}) copy-start(f32[128]{0:T(128)} %copy-done.5) | copy-start | bytes 1540
  169.6 220.8 %copy-start.8 = (f32[128]{0:T(128)S(1)}, f32[128]{0:T(128)}, u32[]{:S(2)}) copy-start(f32[128]{0:T(128)} %copy-done.7) | copy-start | bytes 1540
  169.6 220.8 %copy-start.10 = (f32[128]{0:T(128)S(1)}, f32[128]{0:T(128)}, u32[]{:S(2)}) copy-start(f32[128]{0:T(128)} %copy-done.9) | copy-start | bytes 1540
  169.6 220.8 %copy-start.12 = (f32[128]{0:T(128)S(1)}, f32[128]{0:T(128)}, u32[]{:S(2)}) copy-start(f32[128]{0:T(128)} %copy-done.11) | copy-start | bytes 1540
  169.7 220.8 %copy-start.14 = (f32[128]{0:T(128)S(1)}, f32[128]{0:T(128)}, u32[]{:S(2)}) copy-start(f32[128]{0:T(128)} %copy-done.13) | copy-start | bytes 1540
  169.7 220.8 %copy-start.16 = (f32[128]{0:T(128)S(1)}, f32[128]{0:T(128)}, u32[]{:S(2)}) copy-start(f32[128]{0:T(128)} %copy-done.15) | copy-start | bytes 1540
  169.7 220.8 %copy-start.18 = (f32[128]{0:T(128)S(1)}, f32[128]{0:T(128)}, u32[]{:S(2)}) copy-start(f32[128]{0:T(128)} %copy-done.17) | copy-start | bytes 1540
  169.7 220.8 %copy-start.20 = (f32[128]{0:T(128)S(1)}, f32[128]{0:T(128)}, u32[]{:S(2)}) copy-start(f32[128]{0:T(128)} %copy-done.19) | copy-start | bytes 1540
  169.7 220.8 %copy-start.22 = (f32[128]{0:T(128)S(1)}, f32[128]{0:T(128)}, u32[]{:S(2)}) copy-start(f32[128]{0:T(128)} %copy-done.21) | copy-start | bytes 1540
  383.4 5.8 collective-permute-start.6
  384.7 5.7 collective-permute-start.7
Sparse Core Ops, SparseCore 0:
  12.6 135.0 all-gather.1
  155.7 403.4 reduce-scatter.1
